TPU v7x, 32 devices: a whole 2x2x4 slice. The times are simulated.
32 devices in a mesh: seq: 8 (over z, x), batch: 4 (over y, core).
Axes of the slice: x: 2, y: 2, z: 4, core: 2. Of those that a mesh axis runs over, the one named last changes fastest.
Arguments:
- hidden_in: bfloat16 [16, 1024, 768], P('batch', 'seq'), may hold values from -6 to 6
- lengths: int32 [16], P('batch'), may hold values from 128 to 1024, as said below
- selected: int32 [16, 16, 12, 64], P('batch', 'seq'), may hold values from 0 to 15
- in_proj: bfloat16 [768, 2304], replicated, may hold values from -0.21875 to 0.21875
- scorer: bfloat16 [768, 12], replicated, may hold values from -0.21875 to 0.21875
- out_proj: bfloat16 [768, 768], replicated, may hold values from -0.625 to 0.625
- up_proj: bfloat16 [768, 3072], replicated, may hold values from -0.21875 to 0.21875
- up_bias: bfloat16 [3072], replicated, may hold values from -3 to 3
- down_proj: bfloat16 [3072, 768], replicated, may hold values from -0.109375 to 0.109375
- first_gain: bfloat16 [768], replicated, may hold values from 0.25 to 1.75
- first_shift: bfloat16 [768], replicated, may hold values from -2 to 2
- second_gain: bfloat16 [768], replicated, may hold values from 0.25 to 1.75
- second_shift: bfloat16 [768], replicated, may hold values from -2 to 2
- cotangent: bfloat16 [16, 1024, 768], P('batch', 'seq'), may hold values from -6 to 6
Outputs:
- block_out: bfloat16 [16, 1024, 768], P('batch', 'seq')
- grad_input: bfloat16 [16, 1024, 768], P('batch', 'seq')
- grad_in_proj: float32 [768, 2304], P('seq')
- grad_scorer: float32 [768, 12], P('seq')
- grad_out_proj: float32 [768, 768], P('seq')
- grad_up_proj: float32 [768, 3072], P('seq')
- grad_up_bias: float32 [3072], P('seq')
- grad_down_proj: float32 [3072, 768], P('seq')
- grad_first_gain: float32 [768], P('seq')
- grad_first_shift: float32 [768], P('seq')
- grad_second_gain: float32 [768], P('seq')
- grad_second_shift: float32 [768], P('seq')
Inputs may be any that keep to these rules, and one draw needn't show every extreme that they name: `lengths`: in every group of 4 sequences on one index of batch, one sequence, drawn from the seed, has length 1024.
All inputs are finite; a program needn't handle non-finite values.
Results may differ from a plain program's by a relative error of at most 0.015.
Values may be sent and summed in bfloat16 or wider, within the bound.
A program may use at most 192 MiB of HBM per device.

v0:
```python
from functools import partial
import math

import jax
import jax.numpy as jnp
from jax import lax
from jax.sharding import PartitionSpec as P

TILE = 64
WIN = 64


EPS = 1e-05
NEG = -1e30


def passed_along(block, axis, distance):
    devices = range(lax.axis_size(axis))
    route = [(i - distance, i) for i in devices if i - distance in devices]
    return lax.ppermute(block, axis, route)


def cut_along(value, dim, length):
    before, after = (value.shape[:dim], value.shape[dim + 1 :])
    return jnp.moveaxis(value.reshape(*before, length, -1, *after), dim, 0)


def sum_at_owner(value, axis, dim):
    parts = cut_along(value, dim, lax.axis_size(axis))
    arrived = lax.all_to_all(parts, axis, split_axis=0, concat_axis=0, tiled=True)
    return arrived.astype(jnp.float32).sum(axis=0)


def layer_norm(values, gain, shift):
    average = jnp.mean(values, axis=-1, keepdims=True)
    centered = values - average
    variance = jnp.mean(centered * centered, axis=-1, keepdims=True)
    return centered * lax.rsqrt(variance + EPS) * gain + shift


def window_mask(tile_ids):
    row_index = lax.broadcasted_iota(jnp.int32, (TILE, 2 * TILE), 0)
    col_index = lax.broadcasted_iota(jnp.int32, (TILE, 2 * TILE), 1)
    distance = TILE + row_index - col_index
    inside = (distance >= 0) & (distance <= WIN)
    exists = (tile_ids > 0)[:, None, None] | (col_index >= TILE)[None]
    return inside[None] & exists


def allowed_mask(tile_ids, picks):
    lead = picks.shape[:3]
    near_mask = jnp.broadcast_to(window_mask(tile_ids)[None, :, None], lead + (TILE, 2 * TILE))
    far_mask = picks[:, :, :, None, :] < tile_ids[None, :, None, None, None]
    far_mask = jnp.broadcast_to(far_mask, lead + (TILE, picks.shape[3]))
    return jnp.concatenate([near_mask, far_mask], -1)


def attention_scores(query_tiles, key_window, key_pick, allowed, score_scale):
    near = jnp.einsum(
        "spahd,spbhd->sphab", query_tiles, key_window, preferred_element_type=jnp.float32
    )
    far = jnp.einsum(
        "spahd,sphjd->sphaj", query_tiles, key_pick, preferred_element_type=jnp.float32
    )
    return jnp.where(allowed, jnp.concatenate([near, far], -1) * score_scale, NEG)


def shards(
    hidden_in,
    lengths,
    selected,
    in_proj,
    scorer,
    out_proj,
    up_proj,
    up_bias,
    down_proj,
    first_gain,
    first_shift,
    second_gain,
    second_shift,
    cotangent,
):
    sequences, tokens, model_width = hidden_in.shape
    head_count = scorer.shape[1]
    head_size = model_width // head_count
    tile_count = tokens // TILE
    row_count = sequences * tokens
    span = 2 * TILE
    score_scale = 1.0 / math.sqrt(head_size)
    root_tile = math.sqrt(TILE)
    gain_one = first_gain.astype(jnp.float32)
    shift_one = first_shift.astype(jnp.float32)
    gain_two = second_gain.astype(jnp.float32)
    shift_two = second_shift.astype(jnp.float32)
    hidden = hidden_in.astype(jnp.float32).reshape(row_count, model_width)
    normed = layer_norm(hidden, gain_one, shift_one).astype(jnp.bfloat16)
    packed = jnp.dot(normed, in_proj, preferred_element_type=jnp.float32).astype(jnp.bfloat16)
    weights = jax.nn.sigmoid(jnp.dot(normed, scorer, preferred_element_type=jnp.float32))
    shaped = packed.reshape(sequences, tile_count, TILE, 3, head_count, head_size)
    query_tiles = shaped[:, :, :, 0]
    pair_tiles = shaped[:, :, :, 1:]
    key_float = pair_tiles[:, :, :, 0].astype(jnp.float32)
    value_float = pair_tiles[:, :, :, 1].astype(jnp.float32)
    tile_weights = weights.reshape(sequences, tile_count, TILE, head_count, 1)
    key_comp = jnp.sum(tile_weights * key_float, axis=2) / root_tile
    value_comp = jnp.sum(tile_weights * value_float, axis=2) / root_tile
    compressed = jnp.concatenate(
        [
            key_comp.reshape(sequences, tile_count, model_width),
            value_comp.reshape(sequences, tile_count, model_width),
        ],
        -1,
    ).astype(jnp.bfloat16)
    gathered = lax.all_gather(compressed, "seq", axis=1, tiled=True)
    last_rows = packed.reshape(sequences, tokens, 3 * model_width)[:, tokens - TILE :, model_width:]
    previous = passed_along(last_rows, "seq", 1)
    previous = previous.reshape(sequences, 1, TILE, 2, head_count, head_size)
    before = jnp.concatenate([previous, pair_tiles[:, :-1]], 1)
    window_pairs = jnp.concatenate([before, pair_tiles], 2)
    key_window = window_pairs[:, :, :, 0]
    value_window = window_pairs[:, :, :, 1]
    tile_total = gathered.shape[1]
    choose = (selected[..., None] == jnp.arange(tile_total, dtype=jnp.int32)).astype(jnp.bfloat16)
    gathered_split = gathered.reshape(sequences, tile_total, 2, head_count, head_size)
    key_pick = jnp.einsum(
        "sphjn,snhd->sphjd", choose, gathered_split[:, :, 0], preferred_element_type=jnp.float32
    ).astype(jnp.bfloat16)
    value_pick = jnp.einsum(
        "sphjn,snhd->sphjd", choose, gathered_split[:, :, 1], preferred_element_type=jnp.float32
    ).astype(jnp.bfloat16)
    tile_ids = lax.axis_index("seq") * tile_count + jnp.arange(tile_count, dtype=jnp.int32)
    allowed = allowed_mask(tile_ids, selected)
    scores = attention_scores(query_tiles, key_window, key_pick, allowed, score_scale)
    top_score = jnp.max(scores, -1, keepdims=True)
    log_total = top_score + jnp.log(jnp.sum(jnp.exp(scores - top_score), -1, keepdims=True))
    probs_low = jnp.exp(scores - log_total).astype(jnp.bfloat16)
    near_out = jnp.einsum(
        "sphab,spbhd->spahd",
        probs_low[..., :span],
        value_window,
        preferred_element_type=jnp.float32,
    )
    far_out = jnp.einsum(
        "sphaj,sphjd->spahd", probs_low[..., span:], value_pick, preferred_element_type=jnp.float32
    )
    attended = (near_out + far_out).reshape(row_count, model_width).astype(jnp.bfloat16)
    middle = hidden + jnp.dot(attended, out_proj, preferred_element_type=jnp.float32)
    normed_two = layer_norm(middle, gain_two, shift_two).astype(jnp.bfloat16)
    upper = jnp.dot(normed_two, up_proj, preferred_element_type=jnp.float32) + up_bias.astype(
        jnp.float32
    )
    gelu_fn = partial(jax.nn.gelu, approximate=True)
    active, gelu_pull = jax.vjp(gelu_fn, upper)
    active = active.astype(jnp.bfloat16)
    result = middle + jnp.dot(active, down_proj, preferred_element_type=jnp.float32)
    positions = lax.axis_index("seq") * tokens + jnp.arange(tokens, dtype=jnp.int32)
    valid = (positions[None, :] < lengths[:, None]).reshape(row_count, 1)
    block_out = (
        jnp.where(valid, result, 0.0).astype(jnp.bfloat16).reshape(sequences, tokens, model_width)
    )
    d_result = jnp.where(valid, cotangent.astype(jnp.float32).reshape(row_count, model_width), 0.0)
    d_result_low = d_result.astype(jnp.bfloat16)
    grad_down = jnp.einsum("rf,rd->fd", active, d_result_low, preferred_element_type=jnp.float32)
    d_active = jnp.einsum("rd,fd->rf", d_result_low, down_proj, preferred_element_type=jnp.float32)
    d_upper = gelu_pull(d_active)[0].astype(jnp.bfloat16)
    grad_up = jnp.einsum("rd,rf->df", normed_two, d_upper, preferred_element_type=jnp.float32)
    grad_up_bias = jnp.sum(d_upper.astype(jnp.float32), axis=0)
    d_normed_two = jnp.einsum("rf,df->rd", d_upper, up_proj, preferred_element_type=jnp.float32)
    ignored, norm_two_pull = jax.vjp(layer_norm, middle, gain_two, shift_two)
    d_middle_norm, grad_gain_two, grad_shift_two = norm_two_pull(d_normed_two)
    d_middle = d_result + d_middle_norm
    d_middle_low = d_middle.astype(jnp.bfloat16)
    grad_out = jnp.einsum("rd,re->de", attended, d_middle_low, preferred_element_type=jnp.float32)
    d_attended = jnp.einsum("re,de->rd", d_middle_low, out_proj, preferred_element_type=jnp.float32)
    d_attended = d_attended.astype(jnp.bfloat16).reshape(
        sequences, tile_count, TILE, head_count, head_size
    )
    scores_again = attention_scores(query_tiles, key_window, key_pick, allowed, score_scale)
    probs = jnp.exp(scores_again - log_total)
    probs_again = probs.astype(jnp.bfloat16)
    d_probs_near = jnp.einsum(
        "spahd,spbhd->sphab", d_attended, value_window, preferred_element_type=jnp.float32
    )
    d_probs_far = jnp.einsum(
        "spahd,sphjd->sphaj", d_attended, value_pick, preferred_element_type=jnp.float32
    )
    d_probs = jnp.concatenate([d_probs_near, d_probs_far], -1)
    row_delta = jnp.sum(probs * d_probs, -1, keepdims=True)
    d_scores = (probs * (d_probs - row_delta)).astype(jnp.bfloat16)
    d_near = d_scores[..., :span]
    d_far = d_scores[..., span:]
    d_query = (
        jnp.einsum("sphab,spbhd->spahd", d_near, key_window, preferred_element_type=jnp.float32)
        + jnp.einsum("sphaj,sphjd->spahd", d_far, key_pick, preferred_element_type=jnp.float32)
    ) * score_scale
    d_key_window = (
        jnp.einsum("sphab,spahd->spbhd", d_near, query_tiles, preferred_element_type=jnp.float32)
        * score_scale
    )
    d_value_window = jnp.einsum(
        "sphab,spahd->spbhd",
        probs_again[..., :span],
        d_attended,
        preferred_element_type=jnp.float32,
    )
    d_key_pick = (
        jnp.einsum("sphaj,spahd->sphjd", d_far, query_tiles, preferred_element_type=jnp.float32)
        * score_scale
    )
    d_value_pick = jnp.einsum(
        "sphaj,spahd->sphjd",
        probs_again[..., span:],
        d_attended,
        preferred_element_type=jnp.float32,
    )
    choose_float = choose.astype(jnp.float32)
    d_key_comp = jnp.einsum(
        "sphjn,sphjd->snhd", choose_float, d_key_pick, precision=lax.Precision.HIGHEST
    )
    d_value_comp = jnp.einsum(
        "sphjn,sphjd->snhd", choose_float, d_value_pick, precision=lax.Precision.HIGHEST
    )
    d_compressed = jnp.concatenate(
        [
            d_key_comp.reshape(sequences, tile_total, model_width),
            d_value_comp.reshape(sequences, tile_total, model_width),
        ],
        -1,
    )
    own_comp = sum_at_owner(d_compressed.astype(jnp.bfloat16), "seq", 1)
    own_key_comp = own_comp[..., :model_width].reshape(
        sequences, tile_count, 1, head_count, head_size
    )
    own_value_comp = own_comp[..., model_width:].reshape(
        sequences, tile_count, 1, head_count, head_size
    )
    window_grads = jnp.stack([d_key_window, d_value_window], axis=3)
    back_part = window_grads[:, :, :TILE]
    own_part = window_grads[:, :, TILE:]
    outgoing = back_part[:, 0].reshape(sequences, TILE, 2 * model_width)
    incoming = passed_along(outgoing.astype(jnp.bfloat16), "seq", -1).astype(outgoing.dtype)
    incoming = incoming.reshape(sequences, 1, TILE, 2, head_count, head_size)
    own_total = own_part + jnp.concatenate([back_part[:, 1:], incoming], 1)
    d_key = own_total[:, :, :, 0] + tile_weights * own_key_comp / root_tile
    d_value = own_total[:, :, :, 1] + tile_weights * own_value_comp / root_tile
    d_weights = (
        jnp.sum(key_float * own_key_comp, -1) + jnp.sum(value_float * own_value_comp, -1)
    ) / root_tile
    flat_weights = weights.reshape(sequences, tile_count, TILE, head_count)
    d_logits = (
        (d_weights * flat_weights * (1.0 - flat_weights))
        .reshape(row_count, head_count)
        .astype(jnp.bfloat16)
    )
    d_packed = (
        jnp.stack([d_query, d_key, d_value], axis=3)
        .reshape(row_count, 3 * model_width)
        .astype(jnp.bfloat16)
    )
    grad_in = jnp.einsum("rd,re->de", normed, d_packed, preferred_element_type=jnp.float32)
    grad_score = jnp.einsum("rd,rh->dh", normed, d_logits, preferred_element_type=jnp.float32)
    d_normed = jnp.einsum(
        "re,de->rd", d_packed, in_proj, preferred_element_type=jnp.float32
    ) + jnp.einsum("rh,dh->rd", d_logits, scorer, preferred_element_type=jnp.float32)
    ignored_one, norm_one_pull = jax.vjp(layer_norm, hidden, gain_one, shift_one)
    d_hidden_norm, grad_gain_one, grad_shift_one = norm_one_pull(d_normed)
    grad_input = (
        (d_middle + d_hidden_norm).astype(jnp.bfloat16).reshape(sequences, tokens, model_width)
    )
    all_shares = (
        lax.psum_scatter(grad_in, "seq", scatter_dimension=0, tiled=True),
        lax.psum_scatter(grad_score, "seq", scatter_dimension=0, tiled=True),
        lax.psum_scatter(grad_out, "seq", scatter_dimension=0, tiled=True),
        lax.psum_scatter(grad_up, "seq", scatter_dimension=0, tiled=True),
        lax.psum_scatter(grad_up_bias, "seq", scatter_dimension=0, tiled=True),
        lax.psum_scatter(grad_down, "seq", scatter_dimension=0, tiled=True),
        lax.psum_scatter(grad_gain_one, "seq", scatter_dimension=0, tiled=True),
        lax.psum_scatter(grad_shift_one, "seq", scatter_dimension=0, tiled=True),
        lax.psum_scatter(grad_gain_two, "seq", scatter_dimension=0, tiled=True),
        lax.psum_scatter(grad_shift_two, "seq", scatter_dimension=0, tiled=True),
    )
    ordered = (
        lax.psum(all_shares[0].astype(jnp.bfloat16), "batch").astype(jnp.float32),
        lax.psum(all_shares[1].astype(jnp.bfloat16), "batch").astype(jnp.float32),
        lax.psum(all_shares[2].astype(jnp.bfloat16), "batch").astype(jnp.float32),
        lax.psum(all_shares[3].astype(jnp.bfloat16), "batch").astype(jnp.float32),
        lax.psum(all_shares[4].astype(jnp.bfloat16), "batch").astype(jnp.float32),
        lax.psum(all_shares[5].astype(jnp.bfloat16), "batch").astype(jnp.float32),
        lax.psum(all_shares[6].astype(jnp.bfloat16), "batch").astype(jnp.float32),
        lax.psum(all_shares[7].astype(jnp.bfloat16), "batch").astype(jnp.float32),
        lax.psum(all_shares[8].astype(jnp.bfloat16), "batch").astype(jnp.float32),
        lax.psum(all_shares[9].astype(jnp.bfloat16), "batch").astype(jnp.float32),
    )
    return (
        block_out,
        grad_input,
        ordered[0],
        ordered[1],
        ordered[2],
        ordered[3],
        ordered[4],
        ordered[5],
        ordered[6],
        ordered[7],
        ordered[8],
        ordered[9],
    )


def solution(mesh):
    placed = (
        P("batch", "seq", None),
        P("batch"),
        P("batch", "seq", None, None),
        P(),
        P(),
        P(),
        P(),
        P(),
        P(),
        P(),
        P(),
        P(),
        P(),
        P("batch", "seq", None),
    )
    return jax.shard_map(
        shards,
        mesh=mesh,
        in_specs=placed,
        out_specs=(
            P("batch", "seq", None),
            P("batch", "seq", None),
            P("seq", None),
            P("seq", None),
            P("seq", None),
            P("seq", None),
            P("seq"),
            P("seq", None),
            P("seq"),
            P("seq"),
            P("seq"),
            P("seq"),
        ),
        check_vma=False,
    )
```

profile of v0, /device:TPU:0, one launch (start us, length us, event | category | flops | bytes accessed | tf_op | source)
XLA Modules:
  0.0 985.6 jit_solution(5923777706496326792)
XLA Ops:
  18.7 6.2 collective-permute-start
  24.9 4.3 copy.104
  29.2 9.7 reshape.291
  38.9 3.9 slice.97
  42.9 7.0 slice.95
  49.9 4.5 slice.94
  60.0 10.3 %fusion.15 = (f32[4,2,12,64]{1,0,3,2:T(4,128)}, f32[4,2,12,64]{1,0,3,2:T(4,128)}) fusion(f32[4,2,64,12]{2,1,0,3:T(2,128)} %mul.298, bf16[4,2,64,3,12,64]{2,1,0,5,4,3:T(2,128)(2,1)} %reshape.291), kind=kLoop, calls=%fused_computation.33 | loop fusion | flops 2347008 | bytes 1646592 | tf_op jit(solution)/shard_map/reduce_sum | solution.py:106
  70.3 2.3 copy.110
  74.9 2.5 copy.112
  81.1 32.6 %all_gather.3 = bf16[4,16,1536]{2,0,1:T(4,128)(2,1)} all-gather(bf16[4,2,1536]{2,0,1:T(4,128)(2,1)S(1)} %copy.114), channel_id=1, replica_groups=mesh['seq'=8,'batch'=4] {'seq'}, dimensions={1}, use_global_device_ids=true | all-gather | bytes 221184 | tf_op jit(solution)/shard_map/all_gather | solution.py:115
  117.6 4.9 copy.159
  122.6 4.5 copy.158
  137.8 2.7 fusion.51
  140.5 2.2 fusion.30
  142.8 4.0 reshape.290
  146.7 4.3 copy.106
  151.0 3.8 pad_maximum_fusion.3
  156.1 3.1 copy-done.6
  160.7 3.0 exponential_reduce_fusion
  169.8 2.8 copy.120
  172.5 5.0 convert_element_type.202
  177.5 2.8 fusion.108
  180.7 4.9 fusion.99
  185.8 7.2 convert_reduce_fusion
  193.0 3.5 multiply_reduce_fusion.1
  201.3 2.3 copy.121
  203.6 4.6 reshape.296
  208.3 3.0 fusion.26
  211.6 2.4 fusion.53
  214.0 2.3 fusion.64
  220.5 39.8 %multiply_convert_fusion = bf16[4,2,12,64,192]{4,3,2,1,0:T(8,128)(2,1)S(1)} fusion(f32[4,2,12,64,64]{4,3,2,1,0:T(8,128)} %fusion.64, f32[4,2,12,64,128]{4,3,2,1,0:T(8,128)} %fusion.53, f32[4,2,12,64]{3,2,1,0:T(8,128)} %copy-done.42, f32[4,2,12,64,64]{4,3,2,1,0:T(8,128)} %fusion.30, f32[4,2,12,64,128]{4,3,2,1,0:T(8,128)} %copy-done.7, ...), kind=kOutput, calls=%fused_computation.21 | output fusion | flops 18880704 | bytes 13000704 | tf_op jit(solution)/shard_map/sub | solution.py:190
  267.5 10.6 %all_to_all.5 = bf16[8,4,2,1536]{3,2,1,0:T(2,128)(2,1)S(1)} all-to-all(bf16[8,4,2,1536]{3,2,1,0:T(2,128)(2,1)S(1)} %copy.137), channel_id=1, replica_groups=mesh['seq'=8,'batch'=4] {'seq'}, dimensions={0} | all-to-all | bytes 393216 | tf_op jit(solution)/shard_map/all_to_all | solution.py:30
  280.3 2.4 copy.139
  284.1 2.4 copy.140
  286.5 9.5 fusion.18
  299.6 2.3 fusion.111
  301.9 3.5 fusion.112
  307.1 2.4 fusion.47
  309.5 2.3 multiply_bitcast_fusion
  317.3 5.1 copy.128
  322.4 4.0 convert_element_type.214
  327.9 4.3 fusion.19
  335.8 5.4 collective-permute-done.1
  341.1 4.2 reshape.305
  345.4 5.0 copy.129
  350.4 5.9 fusion.2
  358.3 2.7 maximum_convert_fusion
  361.0 9.3 copy.138
  370.3 11.5 %convert_element_type.217 = bf16[512,2304]{0,1:T(8,128)(2,1)} reshape(bf16[4,2,64,3,12,64]{2,1,0,5,4,3:T(2,128)(2,1)} %copy.138) | data formatting | bytes 4718592 | tf_op jit(solution)/shard_map/convert_element_type | solution.py:259
  381.9 6.9 fusion.110
  389.5 9.0 fusion.98
  398.5 10.3 %fusion.100 = f32[3072,768]{1,0:T(8,128)} fusion(bf16[512,768]{1,0:T(8,128)(2,1)} %fusion.25, f32[512,3072]{1,0:T(8,128)} %copy-done.78, f32[3072]{0:T(1024)} %convert_element_type.206), kind=kOutput, calls=%fused_computation.179 | convolution fusion | flops 2431647744 | bytes 16527360 | tf_op jit(solution)/shard_map/rf,rd->fd/dot_general | solution.py:164
  411.3 9.5 select_convert_fusion
  422.4 3.8 fusion.109
  426.2 2.3 fusion.103
  428.5 13.3 %reduce-scatter.10.cloned.1.call-done = f32[96,768]{1,0:T(8,128)} async-done(((f32[768,768]{1,0:T(8,128)}), f32[96,768]{1,0:T(8,128)}) %reduce-scatter.10.cloned.1.call-update) | async-done | bytes 294928 | tf_op jit(solution)/shard_map/reduce_scatter | solution.py:274
  443.4 130.1 %reduce-scatter.8.cloned.1.call-done = f32[96,2304]{1,0:T(8,128)} async-done(((f32[768,2304]{1,0:T(8,128)}), f32[96,2304]{1,0:T(8,128)}) %reduce-scatter.8.cloned.1.call-update) | async-done | bytes 884752 | tf_op jit(solution)/shard_map/reduce_scatter | solution.py:272
  575.5 164.3 %reduce-scatter.12.cloned.1.call-done = f32[96,3072]{1,0:T(8,128)} async-done(((f32[768,3072]{1,0:T(8,128)}), f32[96,3072]{1,0:T(8,128)}) %reduce-scatter.12.cloned.1.call-update) | async-done | bytes 1179664 | tf_op jit(solution)/shard_map/reduce_scatter | solution.py:275
  741.9 164.2 %reduce-scatter.14.cloned.1.call-done = f32[384,768]{1,0:T(8,128)} async-done(((f32[3072,768]{1,0:T(8,128)}), f32[384,768]{1,0:T(8,128)}) %reduce-scatter.14.cloned.1.call-update) | async-done | bytes 1179664 | tf_op jit(solution)/shard_map/reduce_scatter | solution.py:277
  909.6 2.9 fusion.43
  912.5 36.4 %all-reduce.5 = (bf16[3072]{0:T(1024)(128)(2,1)}, bf16[768]{0:T(1024)(128)(2,1)}, bf16[768]{0:T(1024)(128)(2,1)}, bf16[768]{0:T(1024)(128)(2,1)}, bf16[768]{0:T(1024)(128)(2,1)}) all-reduce(f32[3072]{0:T(1024)} %get-tuple-element.38, f32[768]{0:T(1024)S(1)} %get-tuple-element.18, ...), channel_id=6, replica_groups=mesh['seq'=8,'batch'=4] {'seq'}, use_global_device_ids=true, to_apply=%region_25.26.clone | all-reduce | flops 6144 | bytes 36864
  955.3 6.4 all-reduce.6
  968.9 3.6 add_convert_fusion.1
  972.5 2.2 convert_element_type.229
  (283 shorter events, 114.2 us)
Async XLA Ops:
  7.2 7.1 copy-start
  7.2 413.7 %reduce-scatter.16.cloned.1.call-start = ((), (), s32[]{:S(2)}) async-start(), calls=%async_computation.10 | async-start | bytes 442368
  8.7 3.5 copy-start.58
  8.7 3.5 copy-start.50
  18.7 124.1 %collective-permute-start = (bf16[4,64,1536]{2,1,0:T(8,128)(2,1)}, bf16[4,64,1536]{2,1,0:T(8,128)(2,1)}, u32[]{:S(2)}, u32[]{:S(2)}) collective-permute-start(bf16[4,64,1536]{2,1,0:T(8,128)(2,1)} %slice.93), channel_id=1, source_target_pairs={{0,4},{4,8},{8,12},{12,16},{16,20},{20,24},{24,28},{1,5},{5,9},{9,... | collective-permute-start | bytes 2359304 | tf_op jit(solution)/shard_map/ppermute | solution.py:20
  42.9 7.0 copy-start.5
  122.6 4.5 copy-start.25
  127.1 3.5 copy-start.74
  127.1 4.2 copy-start.75
  127.1 4.3 copy-start.72
  127.1 4.3 copy-start.73
  131.4 65.1 %copy-start.64 = (f32[768]{0:T(1024)}, f32[768]{0:T(1024)S(1)}, u32[]{:S(2)}) copy-start(f32[768]{0:T(1024)S(1)} %convert_element_type.203) | copy-start | bytes 9220
  132.0 8.5 copy-start.1
  132.0 8.5 copy-start.20
  134.2 3.6 copy-start.68
  151.0 3.8 copy-start.2
  154.8 11.4 %copy-start.12 = (bf16[4,2,128,2,12,64]{2,5,4,1,0,3:T(8,128)(2,1)}, bf16[4,2,128,2,12,64]{2,5,4,1,0,3:T(8,128)(2,1)S(1)}, u32[]{:S(2)}) copy-start(bf16[4,2,128,2,12,64]{2,5,4,1,0,3:T(8,128)(2,1)S(1)} %pad_maximum_fusion.3) | copy-start | bytes 9437188
  154.9 4.3 copy-start.6
  155.6 8.1 copy-start.7
  155.8 7.9 copy-start.26
  159.2 4.5 copy-start.27
  166.2 2.5 copy-start.23
  177.5 3.1 copy-start.71
  177.5 8.2 slice-start.2
  180.3 16.2 %copy-start.30 = (f32[512,768]{1,0:T(8,128)}, f32[512,768]{1,0:T(8,128)S(1)}, u32[]{:S(2)}) copy-start(f32[512,768]{1,0:T(8,128)S(1)} %get-tuple-element.51) | copy-start | bytes 4718596
  180.3 16.2 %copy-start.62 = (f32[512]{0:T(512)}, f32[512]{0:T(512)S(1)}, u32[]{:S(2)}) copy-start(f32[512]{0:T(512)S(1)} %broadcast_multiply_fusion) | copy-start | bytes 6148
  180.7 15.9 %copy-start.67 = (f32[512]{0:T(512)}, f32[512]{0:T(512)S(1)}, u32[]{:S(2)}) copy-start(f32[512]{0:T(512)S(1)} %fusion.92) | copy-start | bytes 6148
  180.7 5.0 copy-start.38
  180.7 5.0 copy-start.66
  180.7 5.0 slice-start.3
  180.7 12.2 %slice-start = ((s8[4718592]{0:T(1024)(128)(4,1)}), s8[4194304]{0:T(1024)(128)(4,1)S(1)}, s32[]{:S(2)}) async-start(s8[4718592]{0:T(1024)(128)(4,1)} %bitcast.176), calls=%async_computation.12 | async-start | bytes 8388608
  185.7 7.2 copy-start.78
  185.8 7.2 slice-start.1
  193.0 3.5 copy-start.79
  196.5 3.1 copy-start.76
  208.3 3.0 copy-start.10
  208.3 3.3 copy-start.13
  211.6 2.4 copy-start.24
  214.0 2.3 copy-start.35
  220.5 39.8 %copy-start.3 = (bf16[4,2,64,1,12,64]{5,2,4,1,0,3:T(8,128)(2,1)S(1)}, bf16[4,2,64,1,12,64]{5,2,4,1,0,3:T(8,128)(2,1)}, u32[]{:S(2)}) copy-start(bf16[4,2,64,1,12,64]{5,2,4,1,0,3:T(8,128)(2,1)} %copy.159) | copy-start | bytes 2359300
  301.9 5.2 copy-start.57
  301.9 5.2 copy-start.53
  301.9 5.2 copy-start.59
  301.9 139.9 %reduce-scatter.10.cloned.1.call-start = ((), (), s32[]{:S(2)}) async-start(), calls=%async_computation.7 | async-start | bytes 2654208 | tf_op jit(solution)/shard_map/reduce_scatter | solution.py:274
  305.5 268.1 %reduce-scatter.8.cloned.1.call-start = ((), (), s32[]{:S(2)}) async-start(), calls=%async_computation.6 | async-start | bytes 7962624 | tf_op jit(solution)/shard_map/reduce_scatter | solution.py:272
  305.5 4.0 copy-start.4
  309.5 2.8 copy-start.17
  326.4 5.9 copy-start.14
  326.4 5.9 copy-start.19
  326.4 14.8 %collective-permute-start.1 = (bf16[4,64,1536]{2,1,0:T(8,128)(2,1)}, bf16[4,64,1536]{2,1,0:T(8,128)(2,1)}, u32[]{:S(2)}, u32[]{:S(2)}) collective-permute-start(bf16[4,64,1536]{2,1,0:T(8,128)(2,1)} %convert_element_type.214), channel_id=1, source_target_pairs={{4,0},{8,4},{12,8},{16,12},{20,16},{24,20},{28,24},{5,1},{9,5},{13... | collective-permute-start | bytes 2359304 | tf_op jit(solution)/shard_map/ppermute | solution.py:20
  350.4 5.9 copy-start.39
  350.4 5.9 copy-start.40
  350.4 5.9 copy-start.43
  388.8 351.0 %reduce-scatter.12.cloned.1.call-start = ((), (), s32[]{:S(2)}) async-start(), calls=%async_computation.8 | async-start | bytes 10616832 | tf_op jit(solution)/shard_map/reduce_scatter | solution.py:275
  398.5 507.6 %reduce-scatter.14.cloned.1.call-start = ((), (), s32[]{:S(2)}) async-start(), calls=%async_computation.9 | async-start | bytes 10616832 | tf_op jit(solution)/shard_map/reduce_scatter | solution.py:277
  408.8 2.5 copy-start.70
  408.8 563.6 %all-reduce.10.cloned.1.call-start = ((), (), s32[]{:S(2)}) async-start(), calls=%async_computation.11 | async-start | bytes 3538944 | tf_op jit(solution)/shard_map/psum | solution.py:284
  422.4 3.8 copy-start.15
  422.4 3.8 copy-start.45
  422.4 3.8 copy-start.47
  422.4 3.8 copy-start.51
  443.4 466.2 %copy-start.55 = (f32[512]{0:T(512)S(1)}, f32[512]{0:T(512)}, u32[]{:S(2)}) copy-start(f32[512]{0:T(512)} %copy-done.54) | copy-start | bytes 6148
  972.4 4.4 copy-start.41
  972.4 5.4 copy-start.46
  (28 other events, 36.1 us)
Sparse Core Ops, SparseCore 0:
  302.0 68.2 reduce-scatter.15
  373.7 67.9 reduce-scatter.9
  445.5 128.0 reduce-scatter.7
  577.4 162.3 reduce-scatter.11
  743.7 162.4 reduce-scatter.13
  909.3 45.7 all-reduce.9
where the time goes:
time: 991 us; the launch traced here: 986 us
  waiting for transfers between devices  477 us (48%)
  local copies, waits for them, and re-layouts  161 us (16%)
  other arithmetic  138 us (14%)
  matrix products  98.7 us (10%)
  blocking collectives  86.1 us (9%)
  between operations  16.6 us (2%)
    reduce_scatter x1, waiting for transfers between devices, shards(): lax.psum_scatter(grad_up, 'seq', scatter_dimension=0, tiled=True)  164 us
    reduce_scatter x1, waiting for transfers between devices, shards(): lax.psum_scatter(grad_down, 'seq', scatter_dimension=0, tiled=True)  164 us
    reduce_scatter x1, waiting for transfers between devices, shards(): lax.psum_scatter(grad_in, 'seq', scatter_dimension=0, tiled=True)  130 us
    sub x1, other arithmetic, shards(): d_scores = (probs * (d_probs - row_delta)).astype(jnp.bfloat16)  39.8 us
    unnamed x178, local copies, waits for them, and re-layouts  37 us
    unnamed x1, blocking collectives  36.4 us
    all_gather x1, blocking collectives, shards(): gathered = lax.all_gather(compressed, 'seq', axis=1, tiled=True)  32.6 us
    convert_element_type x2, local copies, waits for them, and re-layouts, shards(): d_packed = jnp.stack([d_query, d_key, d_value], axis=3).reshape(row_count...  20.9 us
  transfers between devices with their start and end apart: 8, of which 5 were waited for; matrix products, arithmetic and copies ran while one was open for 23% of the time, Pallas kernels for 0%

commit v1 on v0

--- a/solution.py
+++ b/solution.py
@@ -4,6 +4,8 @@
 import jax
 import jax.numpy as jnp
 from jax import lax
+from jax.experimental import pallas as pl
+from jax.experimental.pallas import tpu as pltpu
 from jax.sharding import PartitionSpec as P
 
 TILE = 64
@@ -63,6 +65,209 @@
         "spahd,sphjd->sphaj", query_tiles, key_pick, preferred_element_type=jnp.float32
     )
     return jnp.where(allowed, jnp.concatenate([near, far], -1) * score_scale, NEG)
+
+
+MESH_ID = pl.DeviceIdType.MESH
+
+
+class Place:
+    def __init__(self, seq_bits):
+        self.seq = lax.axis_index("seq")
+        self.batch = lax.axis_index("batch")
+        self.bits = {"k": self.batch % 2, "y": self.batch // 2}
+        for i in range(seq_bits):
+            self.bits["b%d" % i] = (self.seq // 2**i) % 2
+
+    def partner(self, dim):
+        flip = 1 - 2 * self.bits[dim]
+        if dim == "k":
+            return (self.seq, self.batch + flip)
+        if dim == "y":
+            return (self.seq, self.batch + 2 * flip)
+        return (self.seq + flip * 2 ** int(dim[1:]), self.batch)
+
+
+def pick(axes, fixed):
+    return tuple(fixed[a] if a in fixed else slice(None) for a in axes)
+
+
+class Flow:
+    def __init__(self, place, axes, order, rows, cols, item, bufs, fin, send, recv):
+        self.place, self.axes = place, axes
+        self.dims = ("k",) + order
+        self.rows, self.cols = rows, cols
+        self.item, self.bufs, self.fin = item, bufs, fin
+        self.send, self.recv = send, recv
+        self.copies = []
+
+    def fixed(self, count):
+        return {d: self.place.bits[d] for d in self.dims[:count]}
+
+    def copy(self, src, dst, dim):
+        j = len(self.copies)
+        cp = pltpu.make_async_remote_copy(
+            src_ref=src,
+            dst_ref=dst,
+            send_sem=self.send.at[j],
+            recv_sem=self.recv.at[j],
+            device_id=self.place.partner(dim),
+            device_id_type=MESH_ID,
+        )
+        cp.start()
+        self.copies.append(cp)
+
+    def add(self, j):
+        fixed = self.fixed(j + 1)
+        free = [a for a in self.axes if a not in fixed]
+        count = 2 ** len(free)
+        last = not free
+
+        def body(i, carry):
+            at = {a: (i // 2**n) % 2 for n, a in enumerate(free)}
+            here = self.item.at[pick(self.axes, {**fixed, **at})]
+            there = self.bufs[j].at[pick(free, at)]
+            total = here[...] + there[...]
+            if last:
+                self.fin[self.place.bits["k"], self.place.bits["y"]] = total
+            else:
+                here[...] = total
+            return carry
+
+        if last:
+            body(0, 0)
+        else:
+            lax.fori_loop(0, count, body, 0)
+
+    def advance(self):
+        j = len(self.copies)
+        bits = self.place.bits
+        if j:
+            self.copies[-1].wait_recv()
+            if j <= 5:
+                self.add(j - 1)
+        if j < 5:
+            dim = self.dims[j]
+            other = {**self.fixed(j), dim: 1 - bits[dim]}
+            self.copy(self.item.at[pick(self.axes, other)], self.bufs[j], dim)
+        elif j == 5:
+            piece = self.fin.at[bits["k"], bits["y"]]
+            self.copy(piece, piece, "y")
+        elif j == 6:
+            self.copy(self.fin.at[bits["k"]], self.fin.at[bits["k"]], "k")
+        else:
+            return True
+        return False
+
+    def finish(self):
+        for cp in self.copies:
+            cp.wait_send()
+
+
+def greet(place, dims):
+    barrier = pltpu.get_barrier_semaphore()
+    for dim in dims:
+        pl.semaphore_signal(barrier, inc=1, device_id=place.partner(dim), device_id_type=MESH_ID)
+    pl.semaphore_wait(barrier, len(dims))
+
+
+def recv_shapes(rows, cols):
+    return [pltpu.VMEM((2,) * (4 - j) + (rows, cols), jnp.bfloat16) for j in range(5)]
+
+
+KCOL = ("k", "b2", "b1", "b0", "y")
+KROW = ("b2", "b1", "b0", "k", "y")
+ORDERS = {"A": ("b0", "y", "b1", "b2"), "B": ("y", "b0", "b1", "b2"), "C": ("b1", "b2", "b0", "y")}
+
+
+def reduce_kernel(plan, *refs):
+    count = len(plan)
+    ins, outs, refs = refs[:count], refs[count : 2 * count], refs[2 * count :]
+    items, refs = refs[:count], refs[count:]
+    bufs, refs = refs[: 5 * count], refs[5 * count :]
+    fins, refs = refs[:count], refs[count:]
+    send, recv, local = refs
+    place = Place(3)
+    loads = []
+    for i in range(count):
+        cp = pltpu.make_async_copy(ins[i], items[i], local.at[i])
+        cp.start()
+        loads.append(cp)
+    greet(place, ("k", "y", "b0", "b1", "b2"))
+    flows = []
+    for i, (axes, order, rows, cols) in enumerate(plan):
+        flows.append(Flow(place, axes, ORDERS[order], rows, cols, items[i], bufs[5 * i : 5 * i + 5], fins[i], send.at[i], recv.at[i]))
+    for i in range(count):
+        loads[i].wait()
+        flows[i].advance()
+    stores = []
+    for step in range(7):
+        for i in range(count):
+            if flows[i].advance():
+                cp = pltpu.make_async_copy(fins[i], outs[i], local.at[i])
+                cp.start()
+                stores.append(cp)
+    for flow in flows:
+        flow.finish()
+    for cp in stores:
+        cp.wait()
+
+
+def reduce_items(items, plan):
+    count = len(plan)
+    scratch = [pltpu.VMEM(item.shape, jnp.bfloat16) for item in items]
+    for axes, order, rows, cols in plan:
+        scratch += recv_shapes(rows, cols)
+    scratch += [pltpu.VMEM((2, 2, rows, cols), jnp.bfloat16) for axes, order, rows, cols in plan]
+    scratch += [pltpu.SemaphoreType.DMA((count, 7)), pltpu.SemaphoreType.DMA((count, 7)), pltpu.SemaphoreType.DMA((count,))]
+    return pl.pallas_call(
+        partial(reduce_kernel, plan),
+        out_shape=[jax.ShapeDtypeStruct((2, 2, rows, cols), jnp.bfloat16) for axes, order, rows, cols in plan],
+        in_specs=[pl.BlockSpec(memory_space=pl.ANY)] * count,
+        out_specs=[pl.BlockSpec(memory_space=pl.ANY)] * count,
+        scratch_shapes=scratch,
+        compiler_params=pltpu.CompilerParams(collective_id=0, has_side_effects=True, vmem_limit_bytes=56 * 2**20),
+        name="reduce",
+    )(*items)
+
+
+def by_columns(grad, width):
+    low = grad.astype(jnp.bfloat16).reshape(2, 2, 2, 2, 48, width // 256, 2, 128)
+    return jnp.transpose(low, (6, 0, 1, 2, 3, 4, 5, 7)).reshape(2, 2, 2, 2, 2, 48, width // 2)
+
+
+def from_columns(fin):
+    width = fin.shape[-1]
+    parts = fin.reshape(2, 2, 48, width // 128, 128)
+    return jnp.transpose(parts, (1, 2, 3, 0, 4)).reshape(96, 2 * width).astype(jnp.float32)
+
+
+def reduce_all(grad_in, grad_score, grad_out, grad_up, grad_up_bias, grad_down, columns):
+    plan, items = [], []
+    down = grad_down.astype(jnp.bfloat16).reshape(8, 3, 128, 768)
+    up = grad_up.reshape(768, 8, 3, 128)
+    for c in range(3):
+        plan.append((KROW, "ABC"[(2 * c) % 3], 32, 768))
+        items.append(down[:, c].reshape(2, 2, 2, 2, 2, 32, 768))
+        plan.append((KCOL, "ABC"[(2 * c + 1) % 3], 48, 512))
+        items.append(by_columns(up[:, :, c].reshape(768, 1024), 1024))
+    plan.append((KCOL, "A", 48, 384))
+    items.append(by_columns(grad_out, 768))
+    for g in range(3):
+        plan.append((KCOL, "BCB"[g], 48, 384))
+        items.append(by_columns(grad_in[:, 768 * g : 768 * g + 768], 768))
+    bias = jnp.transpose(grad_up_bias.reshape(8, 3, 128), (0, 1, 2))
+    right = jnp.zeros((8, 96, 128), jnp.float32).at[:, :3].set(bias).reshape(768, 128)
+    left = jnp.concatenate([grad_score] + [c[:, None] for c in columns] + [jnp.zeros((768, 112), jnp.float32)], 1)
+    plan.append((KCOL, "A", 48, 128))
+    items.append(by_columns(jnp.concatenate([left, right], 1), 256))
+    fins = reduce_items(items, plan)
+    down_out = jnp.stack([fins[2 * c].reshape(128, 768) for c in range(3)], 0).reshape(384, 768).astype(jnp.float32)
+    ups = [from_columns(fins[2 * c + 1]).reshape(96, 8, 1, 128) for c in range(3)]
+    up_out = jnp.concatenate(ups, 2).reshape(96, 3072)
+    out_out = from_columns(fins[6])
+    in_out = jnp.concatenate([from_columns(fins[7 + g]) for g in range(3)], 1)
+    misc = from_columns(fins[10])
+    return (in_out, misc[:, :12], out_out, up_out, misc[:3, 128:].reshape(384), down_out) + tuple(misc[:, 12 + i] for i in range(4))
 
 
 def shards(
@@ -268,6 +473,10 @@
     grad_input = (
         (d_middle + d_hidden_norm).astype(jnp.bfloat16).reshape(sequences, tokens, model_width)
     )
+    grads = (grad_in, grad_score, grad_out, grad_up, grad_up_bias, grad_down)
+    columns = (grad_gain_one, grad_shift_one, grad_gain_two, grad_shift_two)
+    if lax.axis_size("seq") == 8:
+        return (block_out, grad_input) + reduce_all(*grads, columns)
     all_shares = (
         lax.psum_scatter(grad_in, "seq", scatter_dimension=0, tiled=True),
         lax.psum_scatter(grad_score, "seq", scatter_dimension=0, tiled=True),

time: 991 us -> 591 us (0.60)
  waiting for transfers between devices: 477 us -> 0.01 us
  local copies, waits for them, and re-layouts: 161 us -> 261 us
  Pallas kernels: 0 us -> 82.2 us
  blocking collectives: 86.1 us -> 32.8 us
  other arithmetic: 138 us -> 113 us
  matrix products: 98.7 us -> 81.9 us
  between operations: 16.6 us -> 1.96 us
    reduce_scatter x4 -> x0, waiting for transfers between devices: 472 us -> none  [the longest x1 164 us: shards(): lax.psum_scatter(grad_up, 'seq', scatter_dimension=0, tiled=True)]
    pallas_call x0 -> x1, Pallas kernels: none -> 82.2 us  [reduce_items(): pl.pallas_call(partial(reduce_kernel, plan), out_shape=[jax.ShapeDtypeStr...]
    reshape x0 -> x17, local copies, waits for them, and re-layouts: none -> 55.9 us  [the longest x8 27.2 us: by_columns(): grad.astype(jnp.bfloat16).reshape(2, 2, 2, 2, 48, width // 256, 2, 128)]
    unnamed x1 -> x0, blocking collectives: 36.4 us -> none
    convert_element_type x0 -> x18, local copies, waits for them, and re-layouts: none -> 29.5 us  [the longest x16 25.8 us: from_columns(): jnp.transpose(parts, (1, 2, 3, 0, 4)).reshape(96, 2 * width)]
    convert_element_type x14 -> x2, other arithmetic: 20.5 us -> 1.94 us  [the longest x1 1.13 us: reduce_all(): jnp.stack([fins[2 * c].reshape(128, 768) for c in range(3)], 0)]
    slice x0 -> x8, local copies, waits for them, and re-layouts: none -> 17.9 us  [the longest x4 12.4 us: reduce_all(): items.append(by_columns(up[:, :, c].reshape(768, 1024), 1024))]
    unnamed x178 -> x167, local copies, waits for them, and re-layouts: 37 us -> 24.7 us
  transfers between devices with their start and end apart: 8 -> 3, of which waited for: 5 -> 0; matrix products, arithmetic and copies ran while one was open for 23% -> 21% of each run, Pallas kernels for 0% -> 0%
where the time goes in v1:
time: 591 us; the launch traced here: 584 us
  local copies, waits for them, and re-layouts  261 us (44%)
  other arithmetic  113 us (19%)
  Pallas kernels  82.2 us (14%)
  matrix products  81.9 us (14%)
  blocking collectives  32.8 us (6%)
  starting transfers between devices  11.5 us (2%)
    pallas_call x1, Pallas kernels, reduce_items(): pl.pallas_call(partial(reduce_kernel, plan), out_shape=[jax.ShapeDtypeStr...  82.2 us
    sub x1, other arithmetic, shards(): d_scores = (probs * (d_probs - row_delta)).astype(jnp.bfloat16)  33.3 us
    all_gather x1, blocking collectives, shards(): gathered = lax.all_gather(compressed, 'seq', axis=1, tiled=True)  32.8 us
    reshape x8, local copies, waits for them, and re-layouts, by_columns(): grad.astype(jnp.bfloat16).reshape(2, 2, 2, 2, 48, width // 256, 2, 128)  27.2 us
    convert_element_type x16, local copies, waits for them, and re-layouts, from_columns(): jnp.transpose(parts, (1, 2, 3, 0, 4)).reshape(96, 2 * width)  25.8 us
    unnamed x167, local copies, waits for them, and re-layouts  24.7 us
    reshape x6, local copies, waits for them, and re-layouts, by_columns(): jnp.transpose(low, (6, 0, 1, 2, 3, 4, 5, 7))  23.6 us
    convert_element_type x2, local copies, waits for them, and re-layouts, shards(): d_packed = jnp.stack([d_query, d_key, d_value], axis=3).reshape(row_count...  20.7 us
  transfers between devices with their start and end apart: 3, of which 0 were waited for; matrix products, arithmetic and copies ran while one was open for 21% of the time, Pallas kernels for 0%

profile of v1, /device:TPU:0, one launch (start us, length us, event | category | flops | bytes accessed | tf_op | source)
XLA Modules:
  0.0 584.3 jit_solution(9679661815289954774)
XLA Ops:
  10.9 6.2 %collective-permute-start = (bf16[4,64,1536]{2,1,0:T(8,128)(2,1)}, bf16[4,64,1536]{2,1,0:T(8,128)(2,1)}, u32[]{:S(2)}, u32[]{:S(2)}) collective-permute-start(bf16[4,64,1536]{2,1,0:T(8,128)(2,1)} %slice.180), channel_id=1, source_target_pairs={{0,4},{4,8},{8,12},{12,16},{16,20},{20,24},{24,28},{1,5},{5,9},{9,... | collective-permute-start | bytes 2359304 | tf_op jit(solution)/shard_map/ppermute | solution.py:22
  19.8 4.3 copy.232
  29.1 9.7 %reshape.491 = bf16[4,2,64,3,12,64]{2,1,0,5,4,3:T(2,128)(2,1)} reshape(bf16[512,2304]{0,1:T(8,128)(2,1)} %copy.232) | data formatting | bytes 4718592 | tf_op jit(solution)/shard_map/reshape | solution.py:305
  38.8 3.9 slice.184
  42.7 10.5 %fusion.15 = (f32[4,2,12,64]{1,0,3,2:T(4,128)}, f32[4,2,12,64]{1,0,3,2:T(4,128)}) fusion(f32[4,2,64,12]{2,1,0,3:T(2,128)S(1)} %copy-done.43, bf16[4,2,64,3,12,64]{2,1,0,5,4,3:T(2,128)(2,1)} %reshape.491), kind=kLoop, calls=%fused_computation.35 | loop fusion | flops 2347008 | bytes 1646592 | tf_op jit(solution)/shard_map/reduce_sum | solution.py:311
  53.2 4.5 slice.181
  67.2 4.9 copy.315
  82.7 32.8 %all_gather.3 = bf16[4,16,1536]{2,0,1:T(4,128)(2,1)} all-gather(bf16[4,2,1536]{2,0,1:T(4,128)(2,1)S(1)} %copy.242), channel_id=1, replica_groups=mesh['seq'=8,'batch'=4] {'seq'}, dimensions={1}, use_global_device_ids=true | all-gather | bytes 221184 | tf_op jit(solution)/shard_map/all_gather | solution.py:320
  118.7 2.7 fusion.51
  121.4 3.5 copy.313
  131.7 4.0 reshape.490
  135.7 4.3 copy.234
  140.0 3.8 pad_maximum_fusion.3
  145.0 3.1 copy-done.5
  149.6 3.0 exponential_reduce_fusion
  158.7 2.8 copy.248
  161.4 4.8 convert_element_type.288
  166.3 2.8 fusion.110
  169.4 5.1 fusion.98
  174.6 5.0 select_convert_fusion
  179.6 7.2 %fusion.102 = (bf16[3072]{0:T(1024)(128)(2,1)}, bf16[512,3072]{1,0:T(8,128)(2,1)S(1)}) fusion(f32[512,3072]{1,0:T(8,128)S(1)} %fusion.98, f32[3072]{0:T(1024)S(1)} %copy-done.63, bf16[512,768]{1,0:T(8,128)(2,1)S(1)} %copy-done.39, bf16[3072,768]{1,0:T(8,128)(2,1)S(1)} %bitcast.309), kind=kOutput, calls=%fused_computation.201 | convolution fusion | flops 2450519040 | bytes 14960640 | tf_op jit(solution)/shard_map/rd,fd->rf/dot_general | solution.py:370
  186.8 5.5 convolution_convert_fusion.2
  192.3 3.5 multiply_reduce_fusion.1
  195.8 5.0 convolution_convert_fusion.1
  208.0 4.3 reshape.496
  212.3 2.7 fusion.64
  216.3 2.7 fusion.26
  223.3 33.3 %multiply_convert_fusion = bf16[4,2,12,64,192]{4,3,2,1,0:T(8,128)(2,1)S(1)} fusion(f32[4,2,12,64,64]{4,3,2,1,0:T(8,128)S(1)} %fusion.64, f32[4,2,12,64,128]{4,3,2,1,0:T(8,128)S(1)} %fusion.53, f32[4,2,12,64]{3,2,1,0:T(8,128)S(1)} %copy-done.45, f32[4,2,12,64,64]{4,3,2,1,0:T(8,128)S(1)} %copy-done.6, f32[4,2,12,64,128]{4,3,2,1,0:T(8,128)S(1)} %copy-done.8, ...), kind=kOutput, calls=%fused_computation.20 | output fusion | flops 18880704 | bytes 13000704 | tf_op jit(solution)/shard_map/sub | solution.py:395
  256.7 2.6 fusion.55
  260.0 2.6 convolution_multiply_fusion
  269.1 6.6 %copy.270 = bf16[768,3072]{0,1:T(8,128)(2,1)} copy(bf16[768,3072]{1,0:T(8,128)(2,1)} %convolution_convert_fusion.1) | data formatting | bytes 9437184 | tf_op jit(solution)/shard_map/convert.52
  275.8 4.6 fusion.105
  285.3 3.7 reshape.505
  289.1 3.2 copy.374
  292.3 4.1 reshape.506.refs_6_
  296.4 2.6 copy.274
  299.0 2.6 copy.271
  301.6 3.2 copy.370
  309.8 5.1 multiply_bitcast_fusion.1
  321.0 4.0 all-to-all-start
  325.0 5.2 copy.256
  330.2 4.0 convert_element_type.300
  336.1 4.0 copy_bitcast_fusion
  344.8 2.8 copy.268
  350.0 9.5 %fusion.18 = (f32[4,2,64,12]{2,1,0,3:T(2,128)S(1)}, f32[4,2,64,12]{2,1,0,3:T(2,128)S(1)}) fusion(f32[4,2,12,64]{1,0,3,2:T(4,128)} %copy.268, bf16[4,2,64,3,12,64]{2,1,0,5,4,3:T(2,128)(2,1)} %reshape.491, f32[4,2,12,64]{1,0,3,2:T(4,128)} %copy.267), kind=kLoop, calls=%fused_computation.38 | loop fusion | flops 2347008 | bytes 1671168 | tf_op jit(solution)/shard_map/reduce_sum | solution.py:453
  366.5 4.0 reshape.524
  370.6 5.1 copy.257
  375.6 5.8 fusion.2
  383.5 2.7 maximum_convert_fusion
  386.2 9.3 %copy.266 = bf16[4,2,64,3,12,64]{2,1,0,5,4,3:T(2,128)(2,1)} copy(bf16[4,2,64,3,12,64]{2,5,4,1,0,3:T(8,128)(2,1)} %maximum_convert_fusion) | data formatting | bytes 4718592 | tf_op jit(solution)/shard_map/convert_element_type | solution.py:464
  395.6 11.3 %convert_element_type.303 = bf16[512,2304]{0,1:T(8,128)(2,1)} reshape(bf16[4,2,64,3,12,64]{2,1,0,5,4,3:T(2,128)(2,1)} %copy.266) | data formatting | bytes 4718592 | tf_op jit(solution)/shard_map/convert_element_type | solution.py:464
  406.9 3.8 fusion.111
  421.3 4.0 convolution_convert_fusion
  427.1 3.5 reshape.511
  430.7 3.1 copy.371
  433.8 4.1 reshape.512.refs_9_
  437.9 3.5 reshape.509
  441.5 3.1 copy.372
  444.6 4.1 reshape.510.refs_8_
  448.7 3.7 reshape.507
  452.5 3.1 copy.373
  455.6 4.1 reshape.508.refs_7_
  459.8 82.2 %reduce.15 = (bf16[2,2,32,768]{3,2,1,0:T(8,128)(2,1)}, bf16[2,2,48,512]{3,2,1,0:T(8,128)(2,1)}, bf16[2,2,32,768]{3,2,1,0:T(8,128)(2,1)}, bf16[2,2,48,512]{3,2,1,...) custom-call(bf16[2,2,2,2,2,32,768]{6,5,4,3,2,1,0:T(8,128)(2,1)} %bit, ...), custom_call_target="tpu_custom_call" | custom-call | tf_op jit(solution)/shard_map/reduce/pallas_call | solution.py:222
  577.1 2.6 reshape.529
  (300 shorter events, 162.5 us)
Async XLA Ops:
  0.6 5.9 %copy-start = (bf16[768,2304]{1,0:T(8,128)(2,1)S(1)}, bf16[768,2304]{1,0:T(8,128)(2,1)}, u32[]{:S(2)}) copy-start(bf16[768,2304]{1,0:T(8,128)(2,1)} %param.19) | copy-start | bytes 10616836
  2.1 2.9 copy-start.53
  3.6 15.6 %copy-start.55 = (f32[4,128]{1,0:T(4,128)}, f32[4,128]{1,0:T(4,128)S(1)}, u32[]{:S(2)}) copy-start(f32[4,128]{1,0:T(4,128)S(1)} %fusion.44) | copy-start | bytes 6148
  4.4 60.5 %copy-start.47 = (f32[768]{0:T(1024)}, f32[768]{0:T(1024)S(1)}, u32[]{:S(2)}) copy-start(f32[768]{0:T(1024)S(1)} %convert_element_type.273) | copy-start | bytes 9220
  10.9 120.7 %collective-permute-start = (bf16[4,64,1536]{2,1,0:T(8,128)(2,1)}, bf16[4,64,1536]{2,1,0:T(8,128)(2,1)}, u32[]{:S(2)}, u32[]{:S(2)}) collective-permute-start(bf16[4,64,1536]{2,1,0:T(8,128)(2,1)} %slice.180), channel_id=1, source_target_pairs={{0,4},{4,8},{8,12},{12,16},{16,20},{20,24},{24,28},{1,5},{5,9},{9,... | collective-permute-start | bytes 2359304 | tf_op jit(solution)/shard_map/ppermute | solution.py:22
  38.8 3.9 copy-start.43
  42.7 10.5 %copy-start.4 = (bf16[4,2,64,3,12,64]{2,1,0,5,4,3:T(2,128)(2,1)S(1)}, bf16[4,2,64,3,12,64]{2,1,0,5,4,3:T(2,128)(2,1)}, u32[]{:S(2)}) copy-start(bf16[4,2,64,3,12,64]{2,1,0,5,4,3:T(2,128)(2,1)} %reshape.491) | copy-start | bytes 7077892
  57.6 7.2 %copy-start.64 = (f32[4,128]{1,0:T(4,128)S(1)}, f32[4,128]{1,0:T(4,128)}, u32[]{:S(2)}) copy-start(f32[4,128]{1,0:T(4,128)} %fusion.93) | copy-start | bytes 6148
  118.7 6.2 %slice-start = ((bf16[4,2,64,3,12,64]{2,1,0,5,4,3:T(2,128)(2,1)}), bf16[4,2,64,2,12,64]{2,1,0,5,4,3:T(2,128)(2,1)S(1)}, s32[]{:S(2)}) async-start(bf16[4,2,64,3,12,64]{2,1,0,5,4,3:T(2,128)(2,1)} %reshape.491), calls=%async_computation.1 | async-start | bytes 6291456 | tf_op jit(solution)/shard_map/slice | solution.py:307
  124.9 2.5 copy-start.73
  124.9 2.5 copy-start.74
  124.9 2.6 copy-start.31
  124.9 3.7 copy-start.57
  124.9 3.7 copy-start.70
  124.9 3.7 copy-start.71
  124.9 3.8 copy-start.37
  140.0 3.8 copy-start.2
  143.8 11.3 %copy-start.12 = (bf16[4,2,128,2,12,64]{2,5,4,1,0,3:T(8,128)(2,1)}, bf16[4,2,128,2,12,64]{2,5,4,1,0,3:T(8,128)(2,1)S(1)}, u32[]{:S(2)}) copy-start(bf16[4,2,128,2,12,64]{2,5,4,1,0,3:T(8,128)(2,1)S(1)} %pad_maximum_fusion.3) | copy-start | bytes 9437188
  143.8 4.3 copy-start.5
  144.6 8.0 %copy-start.7 = (f32[4,2,12,64,128]{4,3,2,1,0:T(8,128)}, f32[4,2,12,64,128]{4,3,2,1,0:T(8,128)S(1)}, u32[]{:S(2)}) copy-start(f32[4,2,12,64,128]{4,3,2,1,0:T(8,128)S(1)} %fusion.32) | copy-start | bytes 9437188
  144.8 7.8 %copy-start.27 = (pred[4,2,12,64,64]{4,3,2,1,0:T(8,128)(4,1)}, pred[4,2,12,64,64]{4,3,2,1,0:T(8,128)(4,1)S(1)}, u32[]{:S(2)}) copy-start(pred[4,2,12,64,64]{4,3,2,1,0:T(8,128)(4,1)S(1)} %broadcast_in_dim.49) | copy-start | bytes 1179652
  148.1 4.5 copy-start.29
  166.3 3.1 copy-start.62
  166.3 3.1 copy-start.69
  166.3 8.3 %slice-start.3 = ((s8[4718592]{0:T(1024)(128)(4,1)}), s8[4194304]{0:T(1024)(128)(4,1)S(1)}, s32[]{:S(2)}) async-start(s8[4718592]{0:T(1024)(128)(4,1)} %bitcast.308), calls=%async_computation.4 | async-start | bytes 8388608
  169.4 5.2 copy-start.63
  169.4 5.2 copy-start.67
  169.4 5.2 slice-start.4
  174.6 5.0 copy-start.39
  174.6 17.7 %slice-start.5 = ((s8[4718592]{0:T(1024)(128)(4,1)}), s8[4194304]{0:T(1024)(128)(4,1)S(1)}, s32[]{:S(2)}) async-start(s8[4718592]{0:T(1024)(128)(4,1)} %bitcast.310), calls=%async_computation.6 | async-start | bytes 8388608
  179.6 12.7 %slice-start.6 = ((s8[4718592]{0:T(1024)(128)(4,1)}), s8[524288]{0:T(1024)(128)(4,1)S(1)}, s32[]{:S(2)}) async-start(s8[4718592]{0:T(1024)(128)(4,1)} %bitcast.310), calls=%async_computation.7 | async-start | bytes 1048576
  201.5 2.6 copy-start.23
  212.3 2.7 copy-start.11
  212.3 3.3 copy-start.17
  216.2 47.9 %copy-start.9 = (f32[4,2,128,1,12,64]{2,5,4,1,0,3:T(8,128)}, f32[4,2,128,1,12,64]{2,5,4,1,0,3:T(8,128)S(1)}, u32[]{:S(2)}) copy-start(f32[4,2,128,1,12,64]{2,5,4,1,0,3:T(8,128)S(1)} %convolution_bitcast_fusion) | copy-start | bytes 9437188
  216.2 4.2 copy-start.13
  216.3 4.9 copy-start.28
  216.3 4.9 copy-start.30
  216.3 4.9 copy-start.45
  220.4 2.9 copy-start.8
  256.7 3.3 copy-start.18
  256.7 2.6 copy-start.3
  260.0 4.1 copy-start.10
  262.6 3.5 slice-start.1
  301.6 3.2 copy-start.26
  309.8 5.1 copy-start.19
  309.8 5.1 copy-start.38
  321.0 19.2 %all-to-all-start = ((bf16[8,4,2,1536]{3,2,1,0:T(2,128)(2,1)}), bf16[8,4,2,1536]{3,2,1,0:T(2,128)(2,1)}, u32[]{:S(2)}, u32[]{:S(2)}) async-start(bf16[8,4,2,1536]{3,2,1,0:T(2,128)(2,1)} %copy.265), calls=%async_computation | async-start | bytes 393216 | tf_op jit(solution)/shard_map/all_to_all | solution.py:32
  334.2 32.4 %collective-permute-start.1 = (bf16[4,64,1536]{2,1,0:T(8,128)(2,1)}, bf16[4,64,1536]{2,1,0:T(8,128)(2,1)}, u32[]{:S(2)}, u32[]{:S(2)}) collective-permute-start(bf16[4,64,1536]{2,1,0:T(8,128)(2,1)} %convert_element_type.300), channel_id=1, source_target_pairs={{4,0},{8,4},{12,8},{16,12},{20,16},{24,20},{28,24},{5,1},{9,5},{13... | collective-permute-start | bytes 2359304 | tf_op jit(solution)/shard_map/ppermute | solution.py:22
  375.6 5.8 copy-start.41
  375.6 5.8 copy-start.42
  375.6 5.8 %copy-start.46 = (f32[4,2,64,12]{2,3,1,0:T(8,128)S(1)}, f32[4,2,64,12]{2,3,1,0:T(8,128)}, u32[]{:S(2)}) copy-start(f32[4,2,64,12]{2,3,1,0:T(8,128)} %copy.258) | copy-start | bytes 73732
  406.9 3.8 copy-start.14
  406.9 3.8 copy-start.48
  406.9 3.8 copy-start.50
  406.9 3.8 copy-start.51
  406.9 3.8 copy-start.54
  459.7 85.1 %copy-start.65 = (f32[512]{0:T(512)S(1)}, f32[512]{0:T(512)}, u32[]{:S(2)}) copy-start(f32[512]{0:T(512)} %get-tuple-element.101) | copy-start | bytes 6148
  459.7 85.1 %copy-start.15 = (bf16[4,128,768]{2,1,0:T(8,128)(2,1)S(1)}, bf16[4,128,768]{2,1,0:T(8,128)(2,1)}, u32[]{:S(2)}) copy-start(bf16[4,128,768]{2,1,0:T(8,128)(2,1)} %param.16) | copy-start | bytes 2359300
  459.7 85.1 %copy-start.22 = (f32[512,768]{1,0:T(8,128)S(1)}, f32[512,768]{1,0:T(8,128)}, u32[]{:S(2)}) copy-start(f32[512,768]{1,0:T(8,128)} %copy-done.21) | copy-start | bytes 4718596
  459.7 85.1 %copy-start.24 = (f32[512,768]{1,0:T(8,128)S(1)}, f32[512,768]{1,0:T(8,128)}, u32[]{:S(2)}) copy-start(f32[512,768]{1,0:T(8,128)} %copy-done.23) | copy-start | bytes 4718596
  459.7 85.1 %copy-start.33 = (bf16[4,128,768]{2,1,0:T(8,128)(2,1)S(1)}, bf16[4,128,768]{2,1,0:T(8,128)(2,1)}, u32[]{:S(2)}) copy-start(bf16[4,128,768]{2,1,0:T(8,128)(2,1)} %param.29) | copy-start | bytes 2359300
  459.8 85.1 %copy-start.61 = (f32[512]{0:T(512)S(1)}, f32[512]{0:T(512)}, u32[]{:S(2)}) copy-start(f32[512]{0:T(512)} %copy-done.60) | copy-start | bytes 6148
  459.8 85.1 %copy-start.68 = (pred[512]{0:T(512)(128)(4,1)S(1)}, pred[512]{0:T(512)(128)(4,1)}, u32[]{:S(2)}) copy-start(pred[512]{0:T(512)(128)(4,1)} %copy-done.66) | copy-start | bytes 1540
  (21 other events, 31.5 us)
